TPU v7x, 512 devices: a whole 4x8x8 slice. The times are simulated.
512 devices in a mesh: dx: 8 (over z), dy: 8 (over y_hi, x), dz: 8 (over y_lo, core).
Axes of the slice: x: 4, y: 8 (y_hi: 2, y_lo: 4; y = y_hi * 4 + y_lo), z: 8, core: 2. Of those that a mesh axis runs over, the one named last changes fastest.
Arguments:
- node_state: bfloat16 [16, 16, 16, 32, 128], P('dx', 'dy', 'dz'), may hold values from -6 to 6
- mesh_base: int32 [3, 16, 16, 16, 32], P(None, 'dx', 'dy', 'dz'), may hold values from 0 to 255, as said below
- mesh_frac: float32 [3, 16, 16, 16, 32], P(None, 'dx', 'dy', 'dz'), may hold values from 0 to 1
- charge: float32 [16, 16, 16, 32], P('dx', 'dy', 'dz'), may hold values from -0.5 to 0.5
- nbr_code: int32 [16, 16, 16, 32, 128], P('dx', 'dy', 'dz'), may hold values from 0 to 863, as said below
- nbr_count: int32 [16, 16, 16, 32], P('dx', 'dy', 'dz'), may hold values from 32 to 128, as said below
- radial_weight: float32 [8, 128], replicated, may hold values from -2 to 2
- mix_weight: bfloat16 [3, 128, 128], replicated, may hold values from -0.5 to 0.5
- force_weight: float32 [128], replicated, may hold values from -0.5 to 0.5
Outputs:
- node_next: bfloat16 [16, 16, 16, 32, 128], P('dx', 'dy', 'dz')
- forces: float32 [3, 16, 16, 16, 32], P(None, 'dx', 'dy', 'dz')
Inputs may be any that keep to these rules, and one draw needn't show every extreme that they name: `mesh_base`: entry d of an atom in octant (X, Y, Z) lies in the atom's octant: from 32 / 2 times its octant index along d up to 16 more, exclusive. In every octant the first atom sits at the lower end and the second at the upper end in every dimension. `nbr_code`: The first atom of every octant has the largest code in its first slot and 0 in its second. `nbr_count`: slots from the count on are padding. The first atom of every octant has 128 live slots, the second 128 // 4.
All inputs are finite; a program needn't handle non-finite values.
Results may differ from a plain program's by a relative error of at most 0.00095.
The roundings to bfloat16 on the way count: a program that leaves them out, or rounds other values in their place, can miss the bound.
Values may be sent and summed in bfloat16 or wider, within the bound.
A program may use at most 64 MiB of HBM per device.

v0:
```python
import math
import jax
import jax.numpy as jnp
from jax import lax
from jax.sharding import PartitionSpec as P

NB = 8
NBR = 128
MB = 32
KZW = 8
cell_size = 1.13
ewald_beta = 0.625
coulomb = 332.0637
sigma_low = 8.0
sigma_rate = 1.5
highest = lax.Precision.HIGHEST


def with_halo(cells, sides, width):
    for axis, dim in sides:
        count = lax.axis_size(axis)
        head = lax.slice_in_dim(cells, 0, width, axis=dim)
        tail = lax.slice_in_dim(cells, cells.shape[dim] - width, cells.shape[dim], axis=dim)
        cells = jnp.concatenate(
            [
                lax.ppermute(tail, axis, [(i, (i + 1) % count) for i in range(count)]),
                cells,
                lax.ppermute(head, axis, [((i + 1) % count, i) for i in range(count)]),
            ],
            axis=dim,
        )
    return cells


def spline_terms(fraction):
    remainder = 1.0 - fraction
    frac_square = fraction * fraction
    frac_cube = frac_square * fraction
    weights = jnp.stack(
        [
            remainder * remainder * remainder / 6.0,
            (3.0 * frac_cube - 6.0 * frac_square + 4.0) / 6.0,
            (-3.0 * frac_cube + 3.0 * frac_square + 3.0 * fraction + 1.0) / 6.0,
            frac_cube / 6.0,
        ]
    )
    slopes = jnp.stack(
        [
            -0.5 * remainder * remainder,
            1.5 * frac_square - 2.0 * fraction,
            -1.5 * frac_square + fraction + 0.5,
            0.5 * frac_square,
        ]
    )
    return (weights, slopes)


def harmonics(direction):
    unit_x, unit_y, unit_z = (direction[0], direction[1], direction[2])
    root_three = math.sqrt(3.0)
    root_fifteen = math.sqrt(15.0)
    root_five = math.sqrt(5.0)
    return jnp.stack(
        [
            jnp.ones_like(unit_x),
            root_three * unit_x,
            root_three * unit_y,
            root_three * unit_z,
            root_fifteen * unit_x * unit_y,
            root_fifteen * unit_y * unit_z,
            0.5 * root_five * (3.0 * unit_z * unit_z - 1.0),
            root_fifteen * unit_x * unit_z,
            0.5 * root_fifteen * (unit_x * unit_x - unit_y * unit_y),
        ]
    )


def edge_terms(displace, active):
    square = jnp.sum(displace * displace, axis=0)
    direction = displace / jnp.sqrt(square + 1.0)
    angular = harmonics(direction)
    distance = cell_size * jnp.sqrt(square)
    widths = sigma_low * jnp.power(sigma_rate, jnp.arange(NB).astype(jnp.float32))
    radial = jnp.exp(-jnp.square(distance[None] / widths[:, None, None]))
    products = radial[:, None] * angular[None] * active.astype(jnp.float32)[None, None]
    atom_rows = displace.shape[1]
    return jnp.transpose(products, (2, 0, 1, 3)).reshape(atom_rows, NB * 9, -1).astype(jnp.bfloat16)


def node_update(edge_values, neighbour_state, own_state, radial_weight, mix_weight, force_weight):
    summed = jnp.einsum(
        "bkn,bnc->bkc", edge_values, neighbour_state, preferred_element_type=jnp.float32
    )
    atom_rows = summed.shape[0]
    summed = summed.reshape(atom_rows, NB, 9, -1)
    message = (jnp.sum(summed * radial_weight[None, :, None, :], axis=1) / math.sqrt(NBR)).astype(
        jnp.bfloat16
    )
    scalar = jnp.dot(message[:, 0], mix_weight[0], preferred_element_type=jnp.float32)
    vector = jnp.einsum(
        "bmc,cd->bmd", message[:, 1:4], mix_weight[1], preferred_element_type=jnp.float32
    )
    tensor = jnp.einsum(
        "bmc,cd->bmd", message[:, 4:9], mix_weight[2], preferred_element_type=jnp.float32
    )
    invariant = scalar + jnp.sum(tensor * tensor, axis=1)
    gating = jax.nn.sigmoid(invariant)
    updated = (own_state.astype(jnp.float32) + jax.nn.silu(invariant)).astype(jnp.bfloat16)
    short_push = jnp.sum(vector * (gating * force_weight)[:, None, :], axis=2)
    return (updated, jnp.transpose(short_push))


def phases(wavenumber, cell_index, extent):
    return 2.0 * math.pi / extent * jnp.mod(wavenumber * cell_index, extent).astype(jnp.float32)


def cell_table(coeff, local_cells, cell_index):
    table = jnp.zeros((local_cells.shape[0], cell_index.shape[0]), jnp.float32)
    for stencil in range(4):
        match = (cell_index[None, :] == (local_cells + stencil)[:, None]).astype(jnp.float32)
        table = table + coeff[stencil][:, None] * match
    return table


def influence(modes_x, modes_y, modes_z, length_x, length_y, length_z):

    def folded(wavenumber, extent):
        return jnp.where(2 * wavenumber >= extent, wavenumber - extent, wavenumber).astype(
            jnp.float32
        ) / (cell_size * extent)

    wave_square = (
        jnp.square(folded(modes_x, length_x))
        + jnp.square(folded(modes_y, length_y))
        + jnp.square(folded(modes_z, length_z))
    )
    volume = cell_size**3 * length_x * length_y * length_z
    return (
        coulomb
        / (math.pi * volume)
        * jnp.exp(-math.pi**2 * wave_square / ewald_beta**2)
        / wave_square
    )


def shards(
    node_state,
    mesh_base,
    mesh_frac,
    charge,
    nbr_code,
    nbr_count,
    radial_weight,
    mix_weight,
    force_weight,
):
    count_x = lax.axis_size("dx")
    count_y = lax.axis_size("dy")
    count_z = lax.axis_size("dz")
    index_x = lax.axis_index("dx")
    index_y = lax.axis_index("dy")
    index_z = lax.axis_index("dz")
    octants = node_state.shape[3]
    channels = node_state.shape[4]
    atom_total = 8 * octants
    half_block = MB // 2
    block_cells = MB + 3
    length_x = MB * count_x
    length_y = MB * count_y
    length_z = MB * count_z
    places = mesh_base.astype(jnp.float32) + mesh_frac
    halo_state = with_halo(node_state, (("dx", 0), ("dy", 1), ("dz", 2)), 1)
    halo_places = with_halo(places, (("dx", 1), ("dy", 2), ("dz", 3)), 1)
    flat_state = halo_state.reshape(64 * octants, channels)
    flat_places = halo_places.reshape(3, 64 * octants)
    piece_rows = octants // 2
    slot_index = jnp.arange(NBR, dtype=jnp.int32)

    def one_block(inputs):
        block_id, code_rows, count_rows, own_places, state_rows = inputs
        octant = block_id // 2
        corner_x = octant // 4
        corner_y = octant // 2 % 2
        corner_z = octant % 2
        side_code = code_rows // octants
        slot_code = code_rows % octants
        step_x = side_code // 9 - 1
        step_y = side_code // 3 % 3 - 1
        step_z = side_code % 3 - 1
        neighbour = (
            ((corner_x + 1 + step_x) * 4 + corner_y + 1 + step_y) * 4 + corner_z + 1 + step_z
        ) * octants + slot_code
        reach_x = 2 * index_x + corner_x + step_x
        reach_y = 2 * index_y + corner_y + step_y
        reach_z = 2 * index_z + corner_z + step_z
        wrap_shift = jnp.stack(
            [
                (reach_x - jnp.mod(reach_x, 2 * count_x)) * half_block,
                (reach_y - jnp.mod(reach_y, 2 * count_y)) * half_block,
                (reach_z - jnp.mod(reach_z, 2 * count_z)) * half_block,
            ]
        ).astype(jnp.float32)
        displace = flat_places[:, neighbour] + wrap_shift - own_places[:, :, None]
        active = slot_index[None, :] < count_rows[:, None]
        edge_values = edge_terms(displace, active)
        return node_update(
            edge_values, flat_state[neighbour], state_rows, radial_weight, mix_weight, force_weight
        )

    updated, short_push = lax.map(
        one_block,
        (
            jnp.arange(16, dtype=jnp.int32),
            nbr_code.reshape(16, piece_rows, NBR),
            nbr_count.reshape(16, piece_rows),
            jnp.transpose(places.reshape(3, 16, piece_rows), (1, 0, 2)),
            node_state.reshape(16, piece_rows, channels),
        ),
    )
    node_next = updated.reshape(node_state.shape)
    short_force = jnp.transpose(short_push, (1, 0, 2)).reshape(3, atom_total)
    base_rows = mesh_base.reshape(3, atom_total)
    frac_rows = mesh_frac.reshape(3, atom_total)
    charge_rows = charge.reshape(atom_total)
    anchor_x = index_x * MB
    anchor_y = index_y * MB
    anchor_z = index_z * MB
    cell_index = jnp.arange(block_cells, dtype=jnp.int32)
    planes = 1 + jnp.arange(KZW, dtype=jnp.int32)
    rows_dev = MB * KZW // count_z
    row_start = (index_y * count_z + index_z) * rows_dev
    modes_x = jnp.arange(length_x, dtype=jnp.int32)
    weights, slopes = spline_terms(frac_rows)
    table_x = cell_table(weights[:, 0], base_rows[0] - anchor_x, cell_index)
    table_y = cell_table(weights[:, 1], base_rows[1] - anchor_y, cell_index)
    table_z = cell_table(weights[:, 2], base_rows[2] - anchor_z, cell_index)
    angle_z = phases(planes[None, :], (anchor_z + cell_index)[:, None], length_z)
    wave_z_re = jnp.dot(table_z, jnp.cos(angle_z), precision=highest)
    wave_z_im = -jnp.dot(table_z, jnp.sin(angle_z), precision=highest)

    def spread_part(inputs):
        part_x, part_y, part_re, part_im, part_charge = inputs
        left_side = jnp.transpose(part_x * part_charge[:, None])
        right_side = jnp.concatenate(
            [part_y[:, :, None] * part_re[:, None, :], part_y[:, :, None] * part_im[:, None, :]],
            axis=2,
        )
        return jnp.dot(left_side, right_side.reshape(part_x.shape[0], -1), precision=highest)

    spread = jnp.sum(
        lax.map(
            spread_part,
            (
                table_x.reshape(8, octants, block_cells),
                table_y.reshape(8, octants, block_cells),
                wave_z_re.reshape(8, octants, KZW),
                wave_z_im.reshape(8, octants, KZW),
                charge_rows.reshape(8, octants),
            ),
        ),
        axis=0,
    )
    spread = spread.reshape(block_cells, block_cells, 2, KZW)
    spread_re = spread[:, :, 0]
    spread_im = spread[:, :, 1]
    wave_count = lax.axis_size(("dy", "dz")) * rows_dev // KZW
    modes_y = jnp.arange(wave_count, dtype=jnp.int32)
    angle_y = phases(modes_y[None, :], (anchor_y + cell_index)[:, None], length_y)
    cos_y = jnp.cos(angle_y)
    sin_y = jnp.sin(angle_y)
    term_re = jnp.einsum("yk,xyz->kzx", cos_y, spread_re, precision=highest) + jnp.einsum(
        "yk,xyz->kzx", sin_y, spread_im, precision=highest
    )
    term_im = jnp.einsum("yk,xyz->kzx", cos_y, spread_im, precision=highest) - jnp.einsum(
        "yk,xyz->kzx", sin_y, spread_re, precision=highest
    )
    slab_rows = lax.psum_scatter(
        jnp.stack([term_re, term_im], axis=2).reshape(
            lax.axis_size(("dy", "dz")) * rows_dev, 2, block_cells
        ),
        ("dy", "dz"),
        scatter_dimension=0,
        tiled=True,
    )
    received = lax.all_gather(slab_rows[None], "dx", axis=0, tiled=True)
    shard_count = received.shape[0]
    cells_now = (jnp.arange(shard_count, dtype=jnp.int32) * MB)[:, None] + cell_index[None, :]
    angle_x = phases(cells_now.reshape(-1)[:, None], modes_x[None, :], length_x)
    cos_x = jnp.cos(angle_x)
    sin_x = jnp.sin(angle_x)
    lined_up = jnp.transpose(received, (1, 2, 0, 3)).reshape(received.shape[1], 2, -1)
    spec_re = jnp.dot(lined_up[:, 0], cos_x, precision=highest) + jnp.dot(
        lined_up[:, 1], sin_x, precision=highest
    )
    spec_im = jnp.dot(lined_up[:, 1], cos_x, precision=highest) - jnp.dot(
        lined_up[:, 0], sin_x, precision=highest
    )
    spectrum = jnp.stack([spec_re, spec_im], axis=1)
    global_rows = row_start + jnp.arange(rows_dev, dtype=jnp.int32)
    green_table = influence(
        modes_x[None, :],
        (global_rows // KZW)[:, None],
        (global_rows % KZW + 1)[:, None],
        length_x,
        length_y,
        length_z,
    )
    scaled = spectrum * green_table[:, None, :]
    angle_back = phases(modes_x[:, None], (anchor_x + cell_index)[None, :], length_x)
    cos_back = jnp.cos(angle_back)
    sin_back = jnp.sin(angle_back)
    back_re = jnp.dot(scaled[:, 0], cos_back, precision=highest) - jnp.dot(
        scaled[:, 1], sin_back, precision=highest
    )
    back_im = jnp.dot(scaled[:, 0], sin_back, precision=highest) + jnp.dot(
        scaled[:, 1], cos_back, precision=highest
    )
    back_rows = jnp.stack([back_re, back_im], axis=1)
    received = lax.all_gather(back_rows, ("dy", "dz"), axis=0, tiled=True)
    wave_count = received.shape[0] // KZW
    modes_y = jnp.arange(wave_count, dtype=jnp.int32)
    angle_y = phases(modes_y[:, None], (anchor_y + cell_index)[None, :], length_y)
    cos_y = jnp.cos(angle_y)
    sin_y = jnp.sin(angle_y)
    lined_up = received.reshape(wave_count, KZW, 2, block_cells)
    part_re = lined_up[:, :, 0]
    part_im = lined_up[:, :, 1]
    wave_re = jnp.einsum("kzx,ky->zxy", part_re, cos_y, precision=highest) - jnp.einsum(
        "kzx,ky->zxy", part_im, sin_y, precision=highest
    )
    wave_im = jnp.einsum("kzx,ky->zxy", part_re, sin_y, precision=highest) + jnp.einsum(
        "kzx,ky->zxy", part_im, cos_y, precision=highest
    )
    wave_rows = jnp.stack([wave_re, wave_im], axis=1)
    angle_z = phases(planes[:, None], (anchor_z + cell_index)[None, :], length_z)
    potential = 2.0 * (
        jnp.einsum("zxy,zw->xyw", wave_rows[:, 0], jnp.cos(angle_z), precision=highest)
        - jnp.einsum("zxy,zw->xyw", wave_rows[:, 1], jnp.sin(angle_z), precision=highest)
    )
    flat_potential = potential.reshape(block_cells, -1)
    slope_x = cell_table(slopes[:, 0], base_rows[0] - anchor_x, cell_index)
    slope_y = cell_table(slopes[:, 1], base_rows[1] - anchor_y, cell_index)
    slope_z = cell_table(slopes[:, 2], base_rows[2] - anchor_z, cell_index)

    def pull_force(inputs):
        part_x, part_slope_x, part_y, part_slope_y, part_z, part_slope_z = inputs
        values = jnp.dot(part_x, flat_potential, precision=highest).reshape(
            -1, block_cells, block_cells
        )
        tilted = jnp.dot(part_slope_x, flat_potential, precision=highest).reshape(
            -1, block_cells, block_cells
        )
        along_z = jnp.sum(values * part_z[:, None, :], axis=2)
        grad_x = jnp.sum(jnp.sum(tilted * part_z[:, None, :], axis=2) * part_y, axis=1)
        grad_y = jnp.sum(along_z * part_slope_y, axis=1)
        grad_z = jnp.sum(jnp.sum(values * part_slope_z[:, None, :], axis=2) * part_y, axis=1)
        return jnp.stack([grad_x, grad_y, grad_z])

    gradients = lax.map(
        pull_force,
        (
            table_x.reshape(8, octants, block_cells),
            slope_x.reshape(8, octants, block_cells),
            table_y.reshape(8, octants, block_cells),
            slope_y.reshape(8, octants, block_cells),
            table_z.reshape(8, octants, block_cells),
            slope_z.reshape(8, octants, block_cells),
        ),
    )
    long_force = -(charge_rows / cell_size) * jnp.transpose(gradients, (1, 0, 2)).reshape(
        3, atom_total
    )
    forces = (short_force + long_force).reshape(3, 2, 2, 2, octants)
    return (node_next, forces)


def solution(mesh):
    placed = (
        P("dx", "dy", "dz", None, None),
        P(None, "dx", "dy", "dz", None),
        P(None, "dx", "dy", "dz", None),
        P("dx", "dy", "dz", None),
        P("dx", "dy", "dz", None, None),
        P("dx", "dy", "dz", None),
        P(),
        P(),
        P(),
    )
    return jax.shard_map(
        shards,
        mesh=mesh,
        in_specs=placed,
        out_specs=(P("dx", "dy", "dz", None, None), P(None, "dx", "dy", "dz", None)),
        check_vma=False,
    )
```

profile of v0, /device:TPU:1, one launch (start us, length us, event | category | flops | bytes accessed | tf_op | source)
XLA Modules:
  0.0 621.4 jit_solution(17176939823443961220)
XLA Ops:
  12.7 5.2 while.36
  22.0 8.6 %copy.132 = f32[2048,2,35]{2,1,0:T(2,128)} copy(f32[2048,2,35]{2,0,1:T(8,128)S(1)} %pad_maximum_fusion.1) | data formatting | bytes 1146880 | tf_op jit(solution)/shard_map/stack | solution.py:278
  31.3 4.8 collective-permute-start
  36.1 8.6 %collective-permute-start.1 = (f32[3,1,2,2,32]{4,3,2,1,0:T(2,128)S(1)}, f32[3,1,2,2,32]{4,3,2,1,0:T(2,128)S(1)}, u32[]{:S(2)}, u32[]{:S(2)}) collective-permute-start(f32[3,1,2,2,32]{4,3,2,1,0:T(2,128)S(1)} %get-tuple-element.721), channel_id=1, source_target_pairs={{64,0},{128,64},{192,128},{256,192},{320,256},{384,320},{448,384},... | collective-permute-start | bytes 4616 | tf_op jit(solution)/shard_map/ppermute | solution.py:28
  46.7 4.6 collective-permute-start.7
  53.2 3.1 collective-permute-start.2
  56.3 8.4 %collective-permute-start.3 = (f32[3,4,1,2,32]{4,3,2,1,0:T(2,128)S(1)}, f32[3,4,1,2,32]{4,3,2,1,0:T(2,128)S(1)}, u32[]{:S(2)}, u32[]{:S(2)}) collective-permute-start(f32[3,4,1,2,32]{4,3,2,1,0:T(2,128)S(1)} %get-tuple-element.710), channel_id=1, source_target_pairs={{8,0},{16,8},{24,16},{32,24},{40,32},{48,40},{56,48},{0,56},{9,1},... | collective-permute-start | bytes 9224 | tf_op jit(solution)/shard_map/ppermute | solution.py:28
  67.6 9.8 %collective-permute-start.9 = (bf16[4,1,2,32,128]{4,3,2,1,0:T(8,128)(2,1)S(1)}, bf16[4,1,2,32,128]{4,3,2,1,0:T(8,128)(2,1)S(1)}, u32[]{:S(2)}, u32[]{:S(2)}) collective-permute-start(bf16[4,1,2,32,128]{4,3,2,1,0:T(8,128)(2,1)S(1)} %get-tuple-element.704), channel_id=1, source_target_pairs={{8,0},{16,8},{24,16},{32,24},{40,32},{48,40},{56,48},{0,56},{9,1},... | collective-permute-start | bytes 196616 | tf_op jit(solution)/shard_map/ppermute | solution.py:28
  77.5 6.0 collective-permute-start.4
  85.6 3.6 collective-permute-start.10
  89.2 2.6 collective-permute-start.11
  97.5 346.0 %while.38 = (s32[]{:T(128)}, bf16[16,16,128]{2,1,0:T(8,128)(2,1)}, f32[16,3,16]{2,1,0:T(4,128)}, bf16[16,16,128]{2,1,0:T(8,128)(2,1)S(1)}, s32[16]{0:T(128)S(1)}...) while((s32[]{:T(128)}, bf16[16,16,128]{2,1,0:T(8,128)(2,1)}, ...), condition=%wide.region_5.6_spmd.clone, body=%wide.region_0.5_spmd.clone.sunk | while | flops 43745308 | bytes 7252634 | solution.py:210
  101.8 5.5 gather_fusion.1
  110.3 6.2 gather_fusion
  123.4 5.5 gather_fusion.1
  132.0 6.2 gather_fusion
  145.0 5.5 gather_fusion.1
  153.6 6.2 gather_fusion
  166.6 5.5 gather_fusion.1
  175.2 6.2 gather_fusion
  188.3 5.5 gather_fusion.1
  196.8 6.2 gather_fusion
  209.9 5.5 gather_fusion.1
  218.4 6.2 gather_fusion
  231.5 5.5 gather_fusion.1
  240.1 6.2 gather_fusion
  253.1 5.5 gather_fusion.1
  261.7 6.2 gather_fusion
  274.8 5.5 gather_fusion.1
  283.3 6.2 gather_fusion
  296.4 5.5 gather_fusion.1
  304.9 6.2 gather_fusion
  318.0 5.5 gather_fusion.1
  326.6 6.2 gather_fusion
  339.6 5.5 gather_fusion.1
  348.2 6.2 gather_fusion
  361.2 5.5 gather_fusion.1
  369.8 6.2 gather_fusion
  382.8 5.5 gather_fusion.1
  391.4 6.2 gather_fusion
  404.5 5.5 gather_fusion.1
  413.0 6.2 gather_fusion
  426.1 5.5 gather_fusion.1
  434.6 6.2 gather_fusion
  445.1 18.5 %all-gather = f32[256,2,35]{2,1,0:T(2,128)S(1)} all-gather(f32[32,2,35]{2,1,0:T(2,128)S(1)} %constant_dynamic-slice_fusion.6), channel_id=2, replica_groups=mesh['dx'=8,'dy'=8,'dz'=8] {'dx'}, dimensions={0}, use_global_device_ids=true | all-gather | bytes 80640 | tf_op jit(solution)/shard_map/all_gather | solution.py:285
  463.9 2.1 fusion.115
  471.8 85.9 %all_gather.7 = f32[2048,2,35]{2,0,1:T(8,128)S(1)} all-gather(f32[32,2,35]{2,0,1:T(8,128)S(1)} %pad_maximum_fusion.6), channel_id=1, replica_groups=mesh['dx'=8,'dy'=8,'dz'=8] {'dy','dz'}, dimensions={0}, use_global_device_ids=true | all-gather | bytes 582400 | tf_op jit(solution)/shard_map/all_gather | solution.py:319
  564.3 49.6 %while.37 = (s32[]{:T(128)}, f32[8,3,32]{2,1,0:T(4,128)S(1)}, f32[8,32,35]{2,1,0:T(8,128)S(1)}, f32[35,1225]{1,0:T(8,128)S(1)}, f32[8,32,35]{2,1,0:T(8,128)S(1)}...) while((s32[]{:T(128)}, f32[8,3,32]{2,1,0:T(4,128)S(1)}, ...), condition=%wide.region_17.18_spmd, body=%wide.region_10.17_spmd.sunk | while | flops 33166656 | bytes 2277293 | solution.py:359
  565.0 2.7 multiply_reduce_fusion.7
  567.8 2.7 fusion.337
  571.2 2.7 multiply_reduce_fusion.7
  574.0 2.7 fusion.337
  577.4 2.7 multiply_reduce_fusion.7
  580.2 2.7 fusion.337
  583.6 2.7 multiply_reduce_fusion.7
  586.4 2.7 fusion.337
  589.8 2.7 multiply_reduce_fusion.7
  592.6 2.7 fusion.337
  596.0 2.7 multiply_reduce_fusion.7
  598.8 2.7 fusion.337
  602.2 2.7 multiply_reduce_fusion.7
  605.0 2.7 fusion.337
  608.4 2.7 multiply_reduce_fusion.7
  611.2 2.7 fusion.337
  (901 shorter events, 161.5 us)
Async XLA Ops:
  7.2 5.5 copy-start.9
  7.2 437.1 %all-reduce.3.cloned.1.call-start = ((), (), s32[]{:S(2)}) async-start(), calls=%async_computation | async-start | bytes 4194304
  7.2 3.2 copy-start.11
  8.1 2.5 copy-start.13
  30.5 14.2 %copy-start.1 = (bf16[2,2,2,32,128]{4,3,2,1,0:T(8,128)(2,1)S(1)}, bf16[2,2,2,32,128]{4,3,2,1,0:T(8,128)(2,1)}, u32[]{:S(2)}) copy-start(bf16[2,2,2,32,128]{4,3,2,1,0:T(8,128)(2,1)} %param.15) | copy-start | bytes 196612
  30.5 63.2 %copy-start.8 = (s32[2,2,2,32]{3,2,1,0:T(2,128)S(1)}, s32[2,2,2,32]{3,2,1,0:T(2,128)}, u32[]{:S(2)}) copy-start(s32[2,2,2,32]{3,2,1,0:T(2,128)} %param.20) | copy-start | bytes 3076
  31.3 21.8 %collective-permute-start = (f32[3,1,2,2,32]{4,3,2,1,0:T(2,128)S(1)}, f32[3,1,2,2,32]{4,3,2,1,0:T(2,128)S(1)}, u32[]{:S(2)}, u32[]{:S(2)}) collective-permute-start(f32[3,1,2,2,32]{4,3,2,1,0:T(2,128)S(1)} %get-tuple-element.720), channel_id=1, source_target_pairs={{0,64},{64,128},{128,192},{192,256},{256,320},{320,384},{384,448},... | collective-permute-start | bytes 4616 | tf_op jit(solution)/shard_map/ppermute | solution.py:26
  36.1 17.0 %collective-permute-start.1 = (f32[3,1,2,2,32]{4,3,2,1,0:T(2,128)S(1)}, f32[3,1,2,2,32]{4,3,2,1,0:T(2,128)S(1)}, u32[]{:S(2)}, u32[]{:S(2)}) collective-permute-start(f32[3,1,2,2,32]{4,3,2,1,0:T(2,128)S(1)} %get-tuple-element.721), channel_id=1, source_target_pairs={{64,0},{128,64},{192,128},{256,192},{320,256},{384,320},{448,384},... | collective-permute-start | bytes 4616 | tf_op jit(solution)/shard_map/ppermute | solution.py:28
  44.7 20.9 %collective-permute-start.6 = (bf16[1,2,2,32,128]{4,3,2,1,0:T(8,128)(2,1)S(1)}, bf16[1,2,2,32,128]{4,3,2,1,0:T(8,128)(2,1)S(1)}, u32[]{:S(2)}, u32[]{:S(2)}) collective-permute-start(bf16[1,2,2,32,128]{4,3,2,1,0:T(8,128)(2,1)S(1)} %get-tuple-element.706), channel_id=1, source_target_pairs={{0,64},{64,128},{128,192},{192,256},{256,320},{320,384},{384,448},... | collective-permute-start | bytes 98312 | tf_op jit(solution)/shard_map/ppermute | solution.py:26
  46.7 19.0 %collective-permute-start.7 = (bf16[1,2,2,32,128]{4,3,2,1,0:T(8,128)(2,1)S(1)}, bf16[1,2,2,32,128]{4,3,2,1,0:T(8,128)(2,1)S(1)}, u32[]{:S(2)}, u32[]{:S(2)}) collective-permute-start(bf16[1,2,2,32,128]{4,3,2,1,0:T(8,128)(2,1)S(1)} %get-tuple-element.705), channel_id=1, source_target_pairs={{64,0},{128,64},{192,128},{256,192},{320,256},{384,320},{448,384},... | collective-permute-start | bytes 98312 | tf_op jit(solution)/shard_map/ppermute | solution.py:28
  53.2 11.7 %collective-permute-start.2 = (f32[3,4,1,2,32]{4,3,2,1,0:T(2,128)S(1)}, f32[3,4,1,2,32]{4,3,2,1,0:T(2,128)S(1)}, u32[]{:S(2)}, u32[]{:S(2)}) collective-permute-start(f32[3,4,1,2,32]{4,3,2,1,0:T(2,128)S(1)} %get-tuple-element.709), channel_id=1, source_target_pairs={{0,8},{8,16},{16,24},{24,32},{32,40},{40,48},{48,56},{56,0},{1,9},... | collective-permute-start | bytes 9224 | tf_op jit(solution)/shard_map/ppermute | solution.py:26
  56.3 9.3 %collective-permute-start.3 = (f32[3,4,1,2,32]{4,3,2,1,0:T(2,128)S(1)}, f32[3,4,1,2,32]{4,3,2,1,0:T(2,128)S(1)}, u32[]{:S(2)}, u32[]{:S(2)}) collective-permute-start(f32[3,4,1,2,32]{4,3,2,1,0:T(2,128)S(1)} %get-tuple-element.710), channel_id=1, source_target_pairs={{8,0},{16,8},{24,16},{32,24},{40,32},{48,40},{56,48},{0,56},{9,1},... | collective-permute-start | bytes 9224 | tf_op jit(solution)/shard_map/ppermute | solution.py:28
  65.6 31.9 %copy-start.3 = (f32[8,128]{1,0:T(8,128)S(1)}, f32[8,128]{1,0:T(8,128)}, u32[]{:S(2)}) copy-start(f32[8,128]{1,0:T(8,128)} %param.21) | copy-start | bytes 12292
  65.6 31.9 %copy-start.7 = (f32[128]{0:T(128)S(1)}, f32[128]{0:T(128)}, u32[]{:S(2)}) copy-start(f32[128]{0:T(128)} %param.23) | copy-start | bytes 1540
  65.7 19.8 %collective-permute-start.8 = (bf16[4,1,2,32,128]{4,3,2,1,0:T(8,128)(2,1)S(1)}, bf16[4,1,2,32,128]{4,3,2,1,0:T(8,128)(2,1)S(1)}, u32[]{:S(2)}, u32[]{:S(2)}) collective-permute-start(bf16[4,1,2,32,128]{4,3,2,1,0:T(8,128)(2,1)S(1)} %get-tuple-element.703), channel_id=1, source_target_pairs={{0,8},{8,16},{16,24},{24,32},{32,40},{40,48},{48,56},{56,0},{1,9},... | collective-permute-start | bytes 196616 | tf_op jit(solution)/shard_map/ppermute | solution.py:26
  67.6 17.9 %collective-permute-start.9 = (bf16[4,1,2,32,128]{4,3,2,1,0:T(8,128)(2,1)S(1)}, bf16[4,1,2,32,128]{4,3,2,1,0:T(8,128)(2,1)S(1)}, u32[]{:S(2)}, u32[]{:S(2)}) collective-permute-start(bf16[4,1,2,32,128]{4,3,2,1,0:T(8,128)(2,1)S(1)} %get-tuple-element.704), channel_id=1, source_target_pairs={{8,0},{16,8},{24,16},{32,24},{40,32},{48,40},{56,48},{0,56},{9,1},... | collective-permute-start | bytes 196616 | tf_op jit(solution)/shard_map/ppermute | solution.py:28
  77.5 18.7 %collective-permute-start.4 = (f32[3,4,4,1,32]{4,3,2,1,0:T(1,128)S(1)}, f32[3,4,4,1,32]{4,3,2,1,0:T(1,128)S(1)}, u32[]{:S(2)}, u32[]{:S(2)}) collective-permute-start(f32[3,4,4,1,32]{4,3,2,1,0:T(1,128)S(1)} %get-tuple-element.707), channel_id=1, source_target_pairs={{0,1},{1,2},{2,3},{3,4},{4,5},{5,6},{6,7},{7,0},{8,9},{9,10},{10,1... | collective-permute-start | bytes 18440 | tf_op jit(solution)/shard_map/ppermute | solution.py:26
  83.6 12.7 %collective-permute-start.5 = (f32[3,4,4,1,32]{4,3,2,1,0:T(1,128)S(1)}, f32[3,4,4,1,32]{4,3,2,1,0:T(1,128)S(1)}, u32[]{:S(2)}, u32[]{:S(2)}) collective-permute-start(f32[3,4,4,1,32]{4,3,2,1,0:T(1,128)S(1)} %get-tuple-element.708), channel_id=1, source_target_pairs={{1,0},{2,1},{3,2},{4,3},{5,4},{6,5},{7,6},{0,7},{9,8},{10,9},{11,1... | collective-permute-start | bytes 18440 | tf_op jit(solution)/shard_map/ppermute | solution.py:28
  85.6 11.2 %collective-permute-start.10 = (bf16[4,4,1,32,128]{4,3,2,1,0:T(8,128)(2,1)S(1)}, bf16[4,4,1,32,128]{4,3,2,1,0:T(8,128)(2,1)S(1)}, u32[]{:S(2)}, u32[]{:S(2)}) collective-permute-start(bf16[4,4,1,32,128]{4,3,2,1,0:T(8,128)(2,1)S(1)} %get-tuple-element.701), channel_id=1, source_target_pairs={{0,1},{1,2},{2,3},{3,4},{4,5},{5,6},{6,7},{7,0},{8,9},{9,10},{10,1... | collective-permute-start | bytes 393224 | tf_op jit(solution)/shard_map/ppermute | solution.py:26
  89.2 8.1 %collective-permute-start.11 = (bf16[4,4,1,32,128]{4,3,2,1,0:T(8,128)(2,1)S(1)}, bf16[4,4,1,32,128]{4,3,2,1,0:T(8,128)(2,1)S(1)}, u32[]{:S(2)}, u32[]{:S(2)}) collective-permute-start(bf16[4,4,1,32,128]{4,3,2,1,0:T(8,128)(2,1)S(1)} %get-tuple-element.702), channel_id=1, source_target_pairs={{1,0},{2,1},{3,2},{4,3},{5,4},{6,5},{7,6},{0,7},{9,8},{10,9},{11,1... | collective-permute-start | bytes 393224 | tf_op jit(solution)/shard_map/ppermute | solution.py:28
  97.5 3.5 copy-start.15
  116.5 0.9 copy-start
  116.5 2.6 copy-start.16
  119.1 3.5 copy-start.15
  138.1 0.9 copy-start
  138.2 2.6 copy-start.16
  140.7 3.5 copy-start.15
  159.8 2.6 copy-start.16
  162.4 3.5 copy-start.15
  181.4 0.9 copy-start
  181.4 2.6 copy-start.16
  184.0 3.5 copy-start.15
  203.0 2.6 copy-start.16
  205.6 3.5 copy-start.15
  224.6 2.6 copy-start.16
  227.2 3.5 copy-start.15
  246.3 2.6 copy-start.16
  248.9 3.5 copy-start.15
  267.9 0.9 copy-start
  267.9 2.6 copy-start.16
  270.5 3.5 copy-start.15
  289.5 0.9 copy-start
  289.5 2.6 copy-start.16
  292.1 3.5 copy-start.15
  311.1 0.9 copy-start
  311.1 2.6 copy-start.16
  313.7 3.5 copy-start.15
  332.8 2.6 copy-start.16
  335.4 3.5 copy-start.15
  354.4 2.6 copy-start.16
  357.0 3.5 copy-start.15
  376.0 2.6 copy-start.16
  378.6 3.5 copy-start.15
  397.6 2.6 copy-start.16
  400.2 3.5 copy-start.15
  419.2 2.6 copy-start.16
  421.8 3.5 copy-start.15
  440.8 2.6 copy-start.16
  443.5 22.5 %copy-start.10 = (s32[280]{0:T(512)S(1)}, s32[280]{0:T(512)}, u32[]{:S(2)}) copy-start(s32[280]{0:T(512)} %add.995) | copy-start | bytes 3364
  465.9 4.2 copy-start.2
  466.0 4.2 copy-start.17
  558.2 3.0 copy-start.12
  558.3 3.0 copy-start.14
  560.6 3.7 copy-start.6
  (12 other events, 10.4 us)
Sparse Core Ops, SparseCore 0:
  30.7 205.6 all-reduce.2
where the time goes:
time: 626 us; the launch traced here: 621 us
  local copies, waits for them, and re-layouts  270 us (43%)
  blocking collectives  104 us (17%)
  matrix products  85.6 us (14%)
  starting transfers between devices  57.5 us (9%)
  loops' own time  48.7 us (8%)
  other arithmetic  38.5 us (6%)
  between operations  15.4 us (2%)
    gather x16, local copies, waits for them, and re-layouts, one_block(): flat_state[neighbour]  98.9 us
    gather x32, local copies, waits for them, and re-layouts, one_block(): displace = flat_places[:, neighbour] + wrap_shift - own_places[:, :, None]  92.9 us
    all_gather x1, blocking collectives, shards(): received = lax.all_gather(back_rows, ('dy', 'dz'), axis=0, tiled=True)  85.9 us
    another operation x1, loops' own time, shards(): lax.map(one_block, (jnp.arange(16, dtype=jnp.int32), nbr_code.reshape(16,...  47.9 us
    ppermute x6, starting transfers between devices, with_halo(): lax.ppermute(head, axis, [((i + 1) % count, i) for i in range(count)])  36 us
    dynamic_slice x48, local copies, waits for them, and re-layouts, shards(): lax.map(one_block, (jnp.arange(16, dtype=jnp.int32), nbr_code.reshape(16,...  22.2 us
    ppermute x6, starting transfers between devices, with_halo(): lax.ppermute(tail, axis, [(i, (i + 1) % count) for i in range(count)])  21.5 us
    dot_general x8, matrix products, pull_force(): jnp.dot(part_x, flat_potential, precision=highest)  21.3 us
  transfers between devices with their start and end apart: 13, of which 2 were waited for; matrix products, arithmetic and copies ran while one was open for 48% of the time, Pallas kernels for 0%

commit v1 on v0

--- a/solution.py
+++ b/solution.py
@@ -316,7 +316,10 @@
         scaled[:, 1], cos_back, precision=highest
     )
     back_rows = jnp.stack([back_re, back_im], axis=1)
-    received = lax.all_gather(back_rows, ("dy", "dz"), axis=0, tiled=True)
+    received = jnp.concatenate(
+        lax.all_to_all(jnp.stack([back_rows] * lax.axis_size(("dy", "dz"))), ("dy", "dz"), 0, 0),
+        axis=0,
+    )
     wave_count = received.shape[0] // KZW
     modes_y = jnp.arange(wave_count, dtype=jnp.int32)
     angle_y = phases(modes_y[:, None], (anchor_y + cell_index)[None, :], length_y)

time: 626 us -> 712 us (1.14); the launches traced: 621 us -> 699 us
  waiting for transfers between devices: 1.35 us -> 141 us
  blocking collectives: 104 us -> 20.8 us
  starting transfers between devices: 57.5 us -> 74 us
  loops' own time: 48.7 us -> 40.4 us
    unnamed x2, waiting for transfers between devices: 0.03 us -> 139 us
    all_gather x1 -> x0, blocking collectives: 85.9 us -> none  [shards(): received = lax.all_gather(back_rows, ('dy', 'dz'), axis=0, tiled=True)]
    gather x32, local copies, waits for them, and re-layouts: 92.9 us -> 112 us  [one_block(): displace = flat_places[:, neighbour] + wrap_shift - own_places[:, :, None]]
    all_to_all x0 -> x1, starting transfers between devices: none -> 16.3 us  [shards(): lax.all_to_all(jnp.stack([back_rows] * lax.axis_size(('dy', 'dz'))), ('dy...]
    dynamic_slice x48, local copies, waits for them, and re-layouts: 22.2 us -> 9.44 us  [shards(): lax.map(one_block, (jnp.arange(16, dtype=jnp.int32), nbr_code.reshape(16,...]
    another operation x1, loops' own time: 47.9 us -> 39.3 us  [shards(): lax.map(one_block, (jnp.arange(16, dtype=jnp.int32), nbr_code.reshape(16,...]
  transfers between devices with their start and end apart: 13 -> 14, of which waited for: 2 -> 3; matrix products, arithmetic and copies ran while one was open for 48% -> 44% of each run, Pallas kernels for 0% -> 0%
where the time goes in v1:
time: 712 us; the launch traced here: 699 us
  local copies, waits for them, and re-layouts  277 us (39%)
  waiting for transfers between devices  141 us (20%)
  matrix products  90.6 us (13%)
  starting transfers between devices  74 us (10%)
  loops' own time  40.4 us (6%)
  other arithmetic  39.9 us (6%)
  blocking collectives  20.8 us (3%)
  between operations  15.7 us (2%)
    unnamed x2, waiting for transfers between devices  139 us
    gather x32, local copies, waits for them, and re-layouts, one_block(): displace = flat_places[:, neighbour] + wrap_shift - own_places[:, :, None]  112 us
    gather x16, local copies, waits for them, and re-layouts, one_block(): flat_state[neighbour]  98.9 us
    another operation x1, loops' own time, shards(): lax.map(one_block, (jnp.arange(16, dtype=jnp.int32), nbr_code.reshape(16,...  39.3 us
    ppermute x6, starting transfers between devices, with_halo(): lax.ppermute(head, axis, [((i + 1) % count, i) for i in range(count)])  36.2 us
    dot_general x8, matrix products, pull_force(): jnp.dot(part_slope_x, flat_potential, precision=highest)  26.9 us
    ppermute x6, starting transfers between devices, with_halo(): lax.ppermute(tail, axis, [(i, (i + 1) % count) for i in range(count)])  21.5 us
    dot_general x8, matrix products, pull_force(): jnp.dot(part_x, flat_potential, precision=highest)  21.3 us
  transfers between devices with their start and end apart: 14, of which 3 were waited for; matrix products, arithmetic and copies ran while one was open for 44% of the time, Pallas kernels for 0%

profile of v1, /device:TPU:1, one launch (start us, length us, event | category | flops | bytes accessed | tf_op | source)
XLA Modules:
  0.0 699.3 jit_solution(9795395722157677389)
XLA Ops:
  13.3 5.2 while.36
  22.6 8.6 %copy.134 = f32[2048,2,35]{2,1,0:T(2,128)} copy(f32[2048,2,35]{2,0,1:T(8,128)S(1)} %pad_maximum_fusion.1) | data formatting | bytes 1146880 | tf_op jit(solution)/shard_map/stack | solution.py:278
  31.9 4.8 collective-permute-start
  36.7 8.6 %collective-permute-start.1 = (f32[3,1,2,2,32]{4,3,2,1,0:T(2,128)S(1)}, f32[3,1,2,2,32]{4,3,2,1,0:T(2,128)S(1)}, u32[]{:S(2)}, u32[]{:S(2)}) collective-permute-start(f32[3,1,2,2,32]{4,3,2,1,0:T(2,128)S(1)} %get-tuple-element.721), channel_id=1, source_target_pairs={{64,0},{128,64},{192,128},{256,192},{320,256},{384,320},{448,384},... | collective-permute-start | bytes 4616 | tf_op jit(solution)/shard_map/ppermute | solution.py:28
  47.3 4.6 collective-permute-start.7
  53.2 3.1 collective-permute-start.2
  56.3 8.4 %collective-permute-start.3 = (f32[3,4,1,2,32]{4,3,2,1,0:T(2,128)S(1)}, f32[3,4,1,2,32]{4,3,2,1,0:T(2,128)S(1)}, u32[]{:S(2)}, u32[]{:S(2)}) collective-permute-start(f32[3,4,1,2,32]{4,3,2,1,0:T(2,128)S(1)} %get-tuple-element.710), channel_id=1, source_target_pairs={{8,0},{16,8},{24,16},{32,24},{40,32},{48,40},{56,48},{0,56},{9,1},... | collective-permute-start | bytes 9224 | tf_op jit(solution)/shard_map/ppermute | solution.py:28
  67.6 9.8 %collective-permute-start.9 = (bf16[4,1,2,32,128]{4,3,2,1,0:T(8,128)(2,1)S(1)}, bf16[4,1,2,32,128]{4,3,2,1,0:T(8,128)(2,1)S(1)}, u32[]{:S(2)}, u32[]{:S(2)}) collective-permute-start(bf16[4,1,2,32,128]{4,3,2,1,0:T(8,128)(2,1)S(1)} %get-tuple-element.704), channel_id=1, source_target_pairs={{8,0},{16,8},{24,16},{32,24},{40,32},{48,40},{56,48},{0,56},{9,1},... | collective-permute-start | bytes 196616 | tf_op jit(solution)/shard_map/ppermute | solution.py:28
  77.4 6.1 collective-permute-start.4
  85.5 3.6 collective-permute-start.10
  89.2 2.9 collective-permute-start.11
  97.4 139.0 %all-reduce.3.cloned.1.call-done = f32[2048,2,35]{2,1,0:T(2,128)} async-done(((f32[2048,2,35]{2,1,0:T(2,128)}), f32[2048,2,35]{2,1,0:T(2,128)}) %all-reduce.3.cloned.1.call-update) | async-done | bytes 573456
  237.1 20.8 %all-gather = f32[256,2,35]{2,1,0:T(2,128)S(1)} all-gather(f32[32,2,35]{2,1,0:T(2,128)S(1)} %constant_dynamic-slice_fusion.6), channel_id=2, replica_groups=mesh['dx'=8,'dy'=8,'dz'=8] {'dx'}, dimensions={0}, use_global_device_ids=true | all-gather | bytes 80640 | tf_op jit(solution)/shard_map/all_gather | solution.py:285
  265.7 3.4 reshape.1379
  269.1 16.3 %all-to-all-start = ((f32[64,1,2240]{2,1,0:T(1,128)}), f32[64,1,2240]{2,1,0:T(1,128)S(1)}, u32[]{:S(2)}, u32[]{:S(2)}) async-start(f32[64,1,2240]{2,1,0:T(1,128)} %reshape.1379), calls=%async_computation | async-start | bytes 1179648 | tf_op jit(solution)/shard_map/all_to_all | solution.py:320
  285.5 337.7 %while.38 = (s32[]{:T(128)}, bf16[16,16,128]{2,1,0:T(8,128)(2,1)}, f32[16,3,16]{2,1,0:T(4,128)}, bf16[16,16,128]{2,1,0:T(8,128)(2,1)S(1)}, s32[16]{0:T(128)S(1)}...) while((s32[]{:T(128)}, bf16[16,16,128]{2,1,0:T(8,128)(2,1)}, ...), condition=%wide.region_5.6_spmd.clone, body=%wide.region_0.5_spmd.clone.sunk | while | flops 43745308 | bytes 6858822 | solution.py:210
  289.2 6.7 gather_fusion.1
  298.2 6.2 gather_fusion
  310.3 6.7 gather_fusion.1
  319.3 6.2 gather_fusion
  331.4 6.7 gather_fusion.1
  340.4 6.2 gather_fusion
  352.5 6.7 gather_fusion.1
  361.5 6.2 gather_fusion
  373.6 6.7 gather_fusion.1
  382.6 6.2 gather_fusion
  394.6 6.7 gather_fusion.1
  403.7 6.2 gather_fusion
  415.8 6.7 gather_fusion.1
  424.8 6.2 gather_fusion
  436.9 6.7 gather_fusion.1
  445.9 6.2 gather_fusion
  458.0 6.7 gather_fusion.1
  467.0 6.2 gather_fusion
  479.1 6.7 gather_fusion.1
  488.2 6.2 gather_fusion
  500.2 6.7 gather_fusion.1
  509.3 6.2 gather_fusion
  521.3 6.7 gather_fusion.1
  530.4 6.2 gather_fusion
  542.4 6.7 gather_fusion.1
  551.5 6.2 gather_fusion
  563.5 6.7 gather_fusion.1
  572.6 6.2 gather_fusion
  584.6 6.7 gather_fusion.1
  593.7 6.2 gather_fusion
  605.7 6.7 gather_fusion.1
  614.8 6.2 gather_fusion
  626.6 2.7 reshape.1380
  636.1 55.5 %while.37 = (s32[]{:T(128)}, f32[8,3,32]{2,1,0:T(4,128)S(1)}, f32[8,32,35]{2,1,0:T(8,128)}, f32[35,1225]{1,0:T(8,128)S(1)}, f32[8,32,35]{2,1,0:T(8,128)S(1)}, /*...) while((s32[]{:T(128)}, f32[8,3,32]{2,1,0:T(4,128)S(1)}, ...), condition=%wide.region_17.18_spmd, body=%wide.region_10.17_spmd.sunk | while | flops 33166656 | bytes 1720597 | solution.py:362
  639.8 3.4 fusion.337
  643.9 2.7 multiply_reduce_fusion.7
  646.7 3.4 fusion.337
  650.8 2.7 multiply_reduce_fusion.7
  653.6 3.4 fusion.337
  657.7 2.7 multiply_reduce_fusion.7
  660.5 3.4 fusion.337
  664.6 2.7 multiply_reduce_fusion.7
  667.4 3.4 fusion.337
  671.6 2.7 multiply_reduce_fusion.7
  674.4 3.4 fusion.337
  678.5 2.7 multiply_reduce_fusion.7
  681.3 3.4 fusion.337
  688.2 3.4 fusion.337
  (806 shorter events, 151.8 us)
Async XLA Ops:
  7.2 6.1 copy-start.7
  7.2 229.2 %all-reduce.3.cloned.1.call-start = ((), (), s32[]{:S(2)}) async-start(), calls=%async_computation.1 | async-start | bytes 4194304
  7.2 3.2 copy-start.8
  8.1 2.7 copy-start.10
  31.1 0.7 copy-start.3
  31.1 0.7 copy-start.4
  31.1 14.2 %copy-start.1 = (bf16[2,2,2,32,128]{4,3,2,1,0:T(8,128)(2,1)S(1)}, bf16[2,2,2,32,128]{4,3,2,1,0:T(8,128)(2,1)}, u32[]{:S(2)}) copy-start(bf16[2,2,2,32,128]{4,3,2,1,0:T(8,128)(2,1)} %param.15) | copy-start | bytes 196612
  31.1 61.1 %copy-start.6 = (s32[2,2,2,32]{3,2,1,0:T(2,128)S(1)}, s32[2,2,2,32]{3,2,1,0:T(2,128)}, u32[]{:S(2)}) copy-start(s32[2,2,2,32]{3,2,1,0:T(2,128)} %param.20) | copy-start | bytes 3076
  31.9 21.2 %collective-permute-start = (f32[3,1,2,2,32]{4,3,2,1,0:T(2,128)S(1)}, f32[3,1,2,2,32]{4,3,2,1,0:T(2,128)S(1)}, u32[]{:S(2)}, u32[]{:S(2)}) collective-permute-start(f32[3,1,2,2,32]{4,3,2,1,0:T(2,128)S(1)} %get-tuple-element.720), channel_id=1, source_target_pairs={{0,64},{64,128},{128,192},{192,256},{256,320},{320,384},{384,448},... | collective-permute-start | bytes 4616 | tf_op jit(solution)/shard_map/ppermute | solution.py:26
  36.7 16.4 %collective-permute-start.1 = (f32[3,1,2,2,32]{4,3,2,1,0:T(2,128)S(1)}, f32[3,1,2,2,32]{4,3,2,1,0:T(2,128)S(1)}, u32[]{:S(2)}, u32[]{:S(2)}) collective-permute-start(f32[3,1,2,2,32]{4,3,2,1,0:T(2,128)S(1)} %get-tuple-element.721), channel_id=1, source_target_pairs={{64,0},{128,64},{192,128},{256,192},{320,256},{384,320},{448,384},... | collective-permute-start | bytes 4616 | tf_op jit(solution)/shard_map/ppermute | solution.py:28
  45.3 20.3 %collective-permute-start.6 = (bf16[1,2,2,32,128]{4,3,2,1,0:T(8,128)(2,1)S(1)}, bf16[1,2,2,32,128]{4,3,2,1,0:T(8,128)(2,1)S(1)}, u32[]{:S(2)}, u32[]{:S(2)}) collective-permute-start(bf16[1,2,2,32,128]{4,3,2,1,0:T(8,128)(2,1)S(1)} %get-tuple-element.706), channel_id=1, source_target_pairs={{0,64},{64,128},{128,192},{192,256},{256,320},{320,384},{384,448},... | collective-permute-start | bytes 98312 | tf_op jit(solution)/shard_map/ppermute | solution.py:26
  47.3 18.4 %collective-permute-start.7 = (bf16[1,2,2,32,128]{4,3,2,1,0:T(8,128)(2,1)S(1)}, bf16[1,2,2,32,128]{4,3,2,1,0:T(8,128)(2,1)S(1)}, u32[]{:S(2)}, u32[]{:S(2)}) collective-permute-start(bf16[1,2,2,32,128]{4,3,2,1,0:T(8,128)(2,1)S(1)} %get-tuple-element.705), channel_id=1, source_target_pairs={{64,0},{128,64},{192,128},{256,192},{320,256},{384,320},{448,384},... | collective-permute-start | bytes 98312 | tf_op jit(solution)/shard_map/ppermute | solution.py:28
  53.2 11.7 %collective-permute-start.2 = (f32[3,4,1,2,32]{4,3,2,1,0:T(2,128)S(1)}, f32[3,4,1,2,32]{4,3,2,1,0:T(2,128)S(1)}, u32[]{:S(2)}, u32[]{:S(2)}) collective-permute-start(f32[3,4,1,2,32]{4,3,2,1,0:T(2,128)S(1)} %get-tuple-element.709), channel_id=1, source_target_pairs={{0,8},{8,16},{16,24},{24,32},{32,40},{40,48},{48,56},{56,0},{1,9},... | collective-permute-start | bytes 9224 | tf_op jit(solution)/shard_map/ppermute | solution.py:26
  56.3 9.3 %collective-permute-start.3 = (f32[3,4,1,2,32]{4,3,2,1,0:T(2,128)S(1)}, f32[3,4,1,2,32]{4,3,2,1,0:T(2,128)S(1)}, u32[]{:S(2)}, u32[]{:S(2)}) collective-permute-start(f32[3,4,1,2,32]{4,3,2,1,0:T(2,128)S(1)} %get-tuple-element.710), channel_id=1, source_target_pairs={{8,0},{16,8},{24,16},{32,24},{40,32},{48,40},{56,48},{0,56},{9,1},... | collective-permute-start | bytes 9224 | tf_op jit(solution)/shard_map/ppermute | solution.py:28
  65.7 19.7 %collective-permute-start.8 = (bf16[4,1,2,32,128]{4,3,2,1,0:T(8,128)(2,1)S(1)}, bf16[4,1,2,32,128]{4,3,2,1,0:T(8,128)(2,1)S(1)}, u32[]{:S(2)}, u32[]{:S(2)}) collective-permute-start(bf16[4,1,2,32,128]{4,3,2,1,0:T(8,128)(2,1)S(1)} %get-tuple-element.703), channel_id=1, source_target_pairs={{0,8},{8,16},{16,24},{24,32},{32,40},{40,48},{48,56},{56,0},{1,9},... | collective-permute-start | bytes 196616 | tf_op jit(solution)/shard_map/ppermute | solution.py:26
  67.6 17.8 %collective-permute-start.9 = (bf16[4,1,2,32,128]{4,3,2,1,0:T(8,128)(2,1)S(1)}, bf16[4,1,2,32,128]{4,3,2,1,0:T(8,128)(2,1)S(1)}, u32[]{:S(2)}, u32[]{:S(2)}) collective-permute-start(bf16[4,1,2,32,128]{4,3,2,1,0:T(8,128)(2,1)S(1)} %get-tuple-element.704), channel_id=1, source_target_pairs={{8,0},{16,8},{24,16},{32,24},{40,32},{48,40},{56,48},{0,56},{9,1},... | collective-permute-start | bytes 196616 | tf_op jit(solution)/shard_map/ppermute | solution.py:28
  77.4 17.4 %collective-permute-start.4 = (f32[3,4,4,1,32]{4,3,2,1,0:T(1,128)S(1)}, f32[3,4,4,1,32]{4,3,2,1,0:T(1,128)S(1)}, u32[]{:S(2)}, u32[]{:S(2)}) collective-permute-start(f32[3,4,4,1,32]{4,3,2,1,0:T(1,128)S(1)} %get-tuple-element.707), channel_id=1, source_target_pairs={{0,1},{1,2},{2,3},{3,4},{4,5},{5,6},{6,7},{7,0},{8,9},{9,10},{10,1... | collective-permute-start | bytes 18440 | tf_op jit(solution)/shard_map/ppermute | solution.py:26
  83.5 11.4 %collective-permute-start.5 = (f32[3,4,4,1,32]{4,3,2,1,0:T(1,128)S(1)}, f32[3,4,4,1,32]{4,3,2,1,0:T(1,128)S(1)}, u32[]{:S(2)}, u32[]{:S(2)}) collective-permute-start(f32[3,4,4,1,32]{4,3,2,1,0:T(1,128)S(1)} %get-tuple-element.708), channel_id=1, source_target_pairs={{1,0},{2,1},{3,2},{4,3},{5,4},{6,5},{7,6},{0,7},{9,8},{10,9},{11,1... | collective-permute-start | bytes 18440 | tf_op jit(solution)/shard_map/ppermute | solution.py:28
  85.5 10.9 %collective-permute-start.10 = (bf16[4,4,1,32,128]{4,3,2,1,0:T(8,128)(2,1)S(1)}, bf16[4,4,1,32,128]{4,3,2,1,0:T(8,128)(2,1)S(1)}, u32[]{:S(2)}, u32[]{:S(2)}) collective-permute-start(bf16[4,4,1,32,128]{4,3,2,1,0:T(8,128)(2,1)S(1)} %get-tuple-element.701), channel_id=1, source_target_pairs={{0,1},{1,2},{2,3},{3,4},{4,5},{5,6},{6,7},{7,0},{8,9},{9,10},{10,1... | collective-permute-start | bytes 393224 | tf_op jit(solution)/shard_map/ppermute | solution.py:26
  89.2 8.2 %collective-permute-start.11 = (bf16[4,4,1,32,128]{4,3,2,1,0:T(8,128)(2,1)S(1)}, bf16[4,4,1,32,128]{4,3,2,1,0:T(8,128)(2,1)S(1)}, u32[]{:S(2)}, u32[]{:S(2)}) collective-permute-start(bf16[4,4,1,32,128]{4,3,2,1,0:T(8,128)(2,1)S(1)} %get-tuple-element.702), channel_id=1, source_target_pairs={{1,0},{2,1},{3,2},{4,3},{5,4},{6,5},{7,6},{0,7},{9,8},{10,9},{11,1... | collective-permute-start | bytes 393224 | tf_op jit(solution)/shard_map/ppermute | solution.py:28
  265.7 19.8 %copy-start = (bf16[3,128,128]{2,1,0:T(8,128)(2,1)S(1)}, bf16[3,128,128]{2,1,0:T(8,128)(2,1)}, u32[]{:S(2)}) copy-start(bf16[3,128,128]{2,1,0:T(8,128)(2,1)} %param.22) | copy-start | bytes 294916
  265.7 19.8 %copy-start.2 = (f32[8,128]{1,0:T(8,128)S(1)}, f32[8,128]{1,0:T(8,128)}, u32[]{:S(2)}) copy-start(f32[8,128]{1,0:T(8,128)} %param.21) | copy-start | bytes 12292
  265.7 19.8 %copy-start.5 = (f32[128]{0:T(128)S(1)}, f32[128]{0:T(128)}, u32[]{:S(2)}) copy-start(f32[128]{0:T(128)} %param.23) | copy-start | bytes 1540
  269.1 354.9 %all-to-all-start = ((f32[64,1,2240]{2,1,0:T(1,128)}), f32[64,1,2240]{2,1,0:T(1,128)S(1)}, u32[]{:S(2)}, u32[]{:S(2)}) async-start(f32[64,1,2240]{2,1,0:T(1,128)} %reshape.1379), calls=%async_computation | async-start | bytes 1179648 | tf_op jit(solution)/shard_map/all_to_all | solution.py:320
  630.0 3.0 copy-start.9
  630.1 3.0 copy-start.11
Sparse Core Ops, SparseCore 0:
  31.3 205.0 all-reduce.2
